TPU v7x, 512 devices: a whole 4x8x8 slice. The times are simulated.
512 devices in a mesh: region: 16 (over z, core), row: 32 (over x, y).
Axes of the slice: x: 4, y: 8, z: 8, core: 2. Of those that a mesh axis runs over, the one named last changes fastest.
Arguments:
- queries: float32 [64, 512], P('row'), may hold values from -6 to 6
- descriptors: float32 [131072, 512], P(('region', 'row')), may hold values from -6 to 6
- candidates: int32 [64, 64], replicated, may hold values from 0 to 1023
- cluster_perm: int32 [16, 8192], P('region', 'row'), may hold values from 0 to 8191, each once within a row
- tile_vals: float32 [6144, 128, 128], P(('region', 'row')), may hold values from 0 to 1, as said below
- tile_row: int32 [6144], P(('region', 'row')), may hold values from 0 to 1, as said below
- tile_col: int32 [6144], P(('region', 'row')), may hold values from 0 to 67, as said below
Outputs:
- diffused: float32 [64, 131072], P(None, ('region', 'row'))
- residual: float32 [64, 131072], P(None, ('region', 'row'))
Inputs may be any that keep to these rules, and one draw needn't show every extreme that they name: Each row of cluster_perm names every storage position of its region once. tile_row is a row tile of the owning device. In device (region r, row index i) the first 2 tiles are its diagonal tiles in order; the intra-region column tiles lie on row indices i, i + 1, i - 1, i + 3, i - 3, i + 8, i - 8 and i + 32 // 2 (modulo 32). `tile_col`: every device holds tiles with column slots in both neighbouring regions. `tile_vals`: S is symmetric with nonnegative entries and every row of S sums to at most 1.
All inputs are finite; a program needn't handle non-finite values.
Results may differ from a plain program's by a relative error of at most 0.0003.
Values sent between devices are 32-bit elements; how exact they have to be, the bound alone decides.
No kernel may reach another device: no remote copies, remote signals or barrier semaphores. Data moves between devices by JAX's collectives and lax.ppermute only.
A program may use at most 64 MiB of HBM per device.

v0:
```python
import jax
import jax.numpy as jnp
from jax import lax
from jax.sharding import PartitionSpec as P

ITERS = 3


def with_halo(block, sides, width):
    for axis, dim in sides:
        count = lax.axis_size(axis)
        forward = [(i, i + 1) for i in range(count - 1)]
        forward.append((count - 1, 0))
        backward = [(target, source) for source, target in forward]
        low = lax.ppermute(
            lax.slice_in_dim(block, block.shape[dim] - width, None, axis=dim), axis, forward
        )
        high = lax.ppermute(lax.slice_in_dim(block, 0, width, axis=dim), axis, backward)
        block = jnp.concatenate([low, block, high], axis=dim)
    return block


def apply_operator(direction, tile_vals, tile_row, tile_col):
    tile_size = tile_vals.shape[1]
    query_count = direction.shape[0]
    row_count = direction.shape[1]
    per_device = row_count // tile_size
    faces = with_halo(direction[None], (("region", 0),), 1)
    lower_face = faces[0]
    upper_face = faces[2]
    region_field = lax.all_gather(direction, "row", axis=1, tiled=True)
    joined = jnp.concatenate([region_field, lower_face, upper_face], axis=1)
    slots = joined.reshape(query_count, -1, tile_size).transpose(1, 0, 2)
    picked = slots[tile_col]
    products = jnp.einsum("tqc,trc->tqr", picked, tile_vals, precision=lax.Precision.HIGHEST)
    selector = (tile_row[None, :] == jnp.arange(per_device, dtype=jnp.int32)[:, None]).astype(
        jnp.float32
    )
    summed = jnp.einsum("at,tqr->qar", selector, products, precision=lax.Precision.HIGHEST).reshape(
        query_count, row_count
    )
    return direction - 0.9 * summed


def square_sum(residual):
    return lax.psum(jnp.sum(residual * residual, axis=1), ("region", "row"))


def local(queries, descriptors, candidates, cluster_perm, tile_vals, tile_row, tile_col):
    tile_size = tile_vals.shape[1]
    row_count = descriptors.shape[0]
    feature_width = descriptors.shape[1]
    per_device = row_count // tile_size
    n_row = lax.axis_size("row")
    device_id = lax.axis_index("region") * n_row + lax.axis_index("row")
    all_queries = lax.all_gather(queries, "row", axis=0, tiled=True)
    scores = lax.dot_general(
        all_queries,
        descriptors,
        (((1,), (1,)), ((), ())),
        precision=lax.Precision.HIGHEST,
        preferred_element_type=jnp.float32,
    ) * (1.0 / jnp.sqrt(jnp.float32(feature_width)))
    own_blocks = device_id * per_device + jnp.arange(per_device, dtype=jnp.int32)
    member = jnp.any(candidates[:, :, None] == own_blocks[None, None, :], axis=1)
    member_rows = jnp.repeat(member, tile_size, axis=1)
    stored = jnp.where(member_rows, jnp.exp(scores), jnp.float32(0.0))
    region_scores = lax.all_gather(stored, "row", axis=1, tiled=True)
    seeds = jnp.take(region_scores, cluster_perm[0], axis=1)
    diffused = jnp.zeros_like(seeds)
    residual = seeds
    direction = seeds
    norm_now = square_sum(residual)
    for step in range(ITERS):
        image = apply_operator(direction, tile_vals, tile_row, tile_col)
        curve = lax.psum(jnp.sum(direction * image, axis=1), ("region", "row"))
        alpha = norm_now / curve
        diffused = diffused + alpha[:, None] * direction
        residual = residual - alpha[:, None] * image
        if step + 1 < ITERS:
            norm_next = square_sum(residual)
            direction = residual + (norm_next / norm_now)[:, None] * direction
            norm_now = norm_next
    return (diffused, residual)


def solution(mesh):
    in_specs = (
        P("row", None),
        P(("region", "row"), None),
        P(),
        P("region", "row"),
        P(("region", "row"), None, None),
        P(("region", "row")),
        P(("region", "row")),
    )
    out_specs = (P(None, ("region", "row")), P(None, ("region", "row")))
    return jax.shard_map(local, mesh=mesh, in_specs=in_specs, out_specs=out_specs, check_vma=False)
```

profile of v0, /device:TPU:1, one launch (start us, length us, event | category | flops | bytes accessed | tf_op | source)
XLA Modules:
  0.0 883.6 jit_solution(5404740575829851799)
XLA Ops:
  7.2 1.0 compare_reduce_fusion
  8.4 32.4 %all-gather = f32[32,2,512]{2,1,0:T(2,128)S(1)} all-gather(f32[1,2,512]{2,1,0:T(2,128)} %bitcast.164), channel_id=1, replica_groups=mesh['region'=16,'row'=32] {'row'}, dimensions={0}, use_global_device_ids=true | all-gather | bytes 135168 | tf_op jit(solution)/shard_map/all_gather | solution.py:56
  41.0 2.3 fusion.1
  44.7 85.5 %all-gather.6.cloned.1.call-done = f32[64,8192]{1,0:T(8,128)} async-done(((f32[64,256]{1,0:T(8,128)}), f32[64,8192]{1,0:T(8,128)}) %all-gather.6.cloned.1.call-update) | async-done | bytes 2097168 | tf_op jit(solution)/shard_map/all_gather | solution.py:68
  130.2 3.8 copy.83
  134.0 2.9 gather_fusion
  137.9 4.8 collective-permute-start
  142.7 1.3 collective-permute-done
  144.0 2.4 collective-permute-done.1
  146.4 71.2 %all-gather.8.cloned.1.call-done = f32[64,8192]{1,0:T(8,128)} async-done(((f32[64,256]{1,0:T(8,128)}), f32[64,8192]{1,0:T(8,128)}) %all-gather.8.cloned.1.call-update) | async-done | bytes 2097168 | tf_op jit(solution)/shard_map/all_gather | solution.py:31
  217.6 1.9 bitcast_bitcast_fusion.2
  219.5 1.3 gather_fusion.1
  220.9 2.6 fusion.29
  224.2 101.1 %all-reduce = (f32[64]{0:T(128)S(1)}, f32[64]{0:T(128)S(1)}) all-reduce(f32[64]{0:T(128)S(1)} %get-tuple-element.16, f32[64]{0:T(128)S(1)} %multiply_reduce_fusion.3), channel_id=1, replica_groups=mesh['region'=16,'row'=32] {'region','row'}, use_global_device_ids=true, to_apply=%region_2.3 | all-reduce | flops 128 | bytes 1024 | tf_op jit(solution)/shard_map/psum | solution.py:46
  325.5 94.4 %psum.44 = f32[64]{0:T(128)S(1)} all-reduce(f32[64]{0:T(128)S(1)} %multiply_reduce_fusion.2), channel_id=1, replica_groups=mesh['region'=16,'row'=32] {'region','row'}, use_global_device_ids=true, to_apply=%region_6.7 | all-reduce | flops 64 | bytes 512 | tf_op jit(solution)/shard_map/psum | solution.py:46
  421.0 1.2 collective-permute-start.2
  422.1 1.3 collective-permute-done.2
  423.5 2.7 collective-permute-done.3
  426.1 66.5 %all-gather.10.cloned.1.call-done = f32[64,8192]{1,0:T(8,128)} async-done(((f32[64,256]{1,0:T(8,128)}), f32[64,8192]{1,0:T(8,128)}) %all-gather.10.cloned.1.call-update) | async-done | bytes 2097168 | tf_op jit(solution)/shard_map/all_gather | solution.py:31
  492.6 1.9 bitcast_bitcast_fusion.1
  494.5 1.3 gather_fusion.2
  495.9 2.6 fusion.30
  499.3 101.1 %psum.45 = f32[64]{0:T(128)S(1)} all-reduce(f32[64]{0:T(128)S(1)} %multiply_reduce_fusion.1), channel_id=1, replica_groups=mesh['region'=16,'row'=32] {'region','row'}, use_global_device_ids=true, to_apply=%region_8.9 | all-reduce | flops 64 | bytes 512 | tf_op jit(solution)/shard_map/psum | solution.py:76
  600.6 94.4 %psum.46 = f32[64]{0:T(128)S(1)} all-reduce(f32[64]{0:T(128)S(1)} %multiply_reduce_fusion), channel_id=1, replica_groups=mesh['region'=16,'row'=32] {'region','row'}, use_global_device_ids=true, to_apply=%region_10.11 | all-reduce | flops 64 | bytes 512 | tf_op jit(solution)/shard_map/psum | solution.py:46
  696.6 1.2 collective-permute-start.4
  697.7 1.3 collective-permute-done.4
  699.1 2.7 collective-permute-done.5
  701.7 66.6 %all-gather.12.cloned.1.call-done = f32[64,8192]{1,0:T(8,128)} async-done(((f32[64,256]{1,0:T(8,128)}), f32[64,8192]{1,0:T(8,128)}) %all-gather.12.cloned.1.call-update) | async-done | bytes 2097168 | tf_op jit(solution)/shard_map/all_gather | solution.py:31
  768.3 1.9 bitcast_bitcast_fusion
  770.2 1.6 gather_fusion.3
  771.8 2.6 fusion.31
  775.2 101.1 %psum.47 = f32[64]{0:T(128)S(1)} all-reduce(f32[64]{0:T(128)S(1)} %fusion.8), channel_id=1, replica_groups=mesh['region'=16,'row'=32] {'region','row'}, use_global_device_ids=true, to_apply=%region_12.13 | all-reduce | flops 64 | bytes 512 | tf_op jit(solution)/shard_map/psum | solution.py:76
  (78 shorter events, 8.8 us)
Async XLA Ops:
  7.2 213.7 %copy-start = (f32[12,128,128]{2,1,0:T(8,128)S(1)}, f32[12,128,128]{2,1,0:T(8,128)}, u32[]{:S(2)}) copy-start(f32[12,128,128]{2,1,0:T(8,128)} %param.11) | copy-start | bytes 2359300
  7.2 123.1 %all-gather.6.cloned.1.call-start = ((), (), s32[]{:S(2)}) async-start(), calls=%async_computation | async-start | bytes 2162688 | tf_op jit(solution)/shard_map/all_gather | solution.py:68
  43.3 174.3 %all-gather.8.cloned.1.call-start = ((), (), s32[]{:S(2)}) async-start(), calls=%async_computation.1 | async-start | bytes 2162688 | tf_op jit(solution)/shard_map/all_gather | solution.py:31
  44.7 376.1 %copy-start.4 = (pred[256]{0:T(512)(128)(4,1)}, pred[256]{0:T(512)(128)(4,1)S(1)}, u32[]{:S(2)}) copy-start(pred[256]{0:T(512)(128)(4,1)S(1)} %compare_and_fusion.1) | copy-start | bytes 772
  44.7 93.1 %copy-start.12 = (s32[12]{0:T(128)S(1)}, s32[12]{0:T(128)}, u32[]{:S(2)}) copy-start(s32[12]{0:T(128)} %param.13) | copy-start | bytes 148
  44.7 93.1 %copy-start.11 = (s32[1,256]{1,0:T(1,128)S(1)}, s32[1,256]{1,0:T(1,128)}, u32[]{:S(2)}) copy-start(s32[1,256]{1,0:T(1,128)} %param.10) | copy-start | bytes 3076
  137.8 354.8 %all-gather.10.cloned.1.call-start = ((), (), s32[]{:S(2)}) async-start(), calls=%async_computation.2 | async-start | bytes 2162688 | tf_op jit(solution)/shard_map/all_gather | solution.py:31
  137.9 6.1 collective-permute-start
  142.7 3.7 collective-permute-start.1
  142.7 351.8 %copy-start.6 = (s32[1024]{0:T(1024)}, s32[1024]{0:T(1024)S(1)}, u32[]{:S(2)}) copy-start(s32[1024]{0:T(1024)S(1)} %pad_clamp_fusion) | copy-start | bytes 12292
  219.5 4.0 copy-start.9
  219.5 200.4 %copy-start.1 = (f32[64,256]{1,0:T(8,128)S(1)}, f32[64,256]{1,0:T(8,128)}, u32[]{:S(2)}) copy-start(f32[64,256]{1,0:T(8,128)} %get-tuple-element.17) | copy-start | bytes 196612
  420.7 347.6 %all-gather.12.cloned.1.call-start = ((), (), s32[]{:S(2)}) async-start(), calls=%async_computation.3 | async-start | bytes 2162688 | tf_op jit(solution)/shard_map/all_gather | solution.py:31
  421.0 2.5 collective-permute-start.2
  422.1 4.0 collective-permute-start.3
  494.5 201.1 %copy-start.2 = (f32[64,256]{1,0:T(8,128)S(1)}, f32[64,256]{1,0:T(8,128)}, u32[]{:S(2)}) copy-start(f32[64,256]{1,0:T(8,128)} %multiply_add_fusion.4) | copy-start | bytes 196612
  495.9 200.6 %copy-start.5 = (pred[256]{0:T(512)(128)(4,1)S(1)}, pred[256]{0:T(512)(128)(4,1)}, u32[]{:S(2)}) copy-start(pred[256]{0:T(512)(128)(4,1)} %copy-done.4) | copy-start | bytes 772
  695.0 0.6 copy-start.13
  695.6 72.7 %copy-start.7 = (f32[64]{0:T(128)}, f32[64]{0:T(128)S(1)}, u32[]{:S(2)}) copy-start(f32[64]{0:T(128)S(1)} %div.18) | copy-start | bytes 772
  696.6 2.5 collective-permute-start.4
  697.7 4.0 collective-permute-start.5
  770.2 4.3 copy-start.10
  770.2 4.9 copy-start.8
  770.2 106.2 %copy-start.14 = (f32[64]{0:T(128)S(1)}, f32[64]{0:T(128)}, u32[]{:S(2)}) copy-start(f32[64]{0:T(128)} %copy-done.13) | copy-start | bytes 772
  770.2 106.2 %copy-start.3 = (f32[64,256]{1,0:T(8,128)S(1)}, f32[64,256]{1,0:T(8,128)}, u32[]{:S(2)}) copy-start(f32[64,256]{1,0:T(8,128)} %get-tuple-element.14) | copy-start | bytes 196612
Sparse Core Ops, SparseCore 0:
  43.4 86.7 all-gather.5
  137.9 79.6 all-gather.7
  420.8 71.7 all-gather.9
  696.4 71.7 all-gather.11
where the time goes:
time: 884 us
  blocking collectives  524 us (59%)
  waiting for transfers between devices  302 us (34%)
  between operations  14.1 us (2%)
  local copies, waits for them, and re-layouts  12.2 us (1%)
  other arithmetic  12.1 us (1%)
  matrix products  12 us (1%)
    psum x3, blocking collectives, square_sum(): return lax.psum(jnp.sum(residual * residual, axis=1), ('region', 'row'))  290 us
    all_gather x3, waiting for transfers between devices, apply_operator(): region_field = lax.all_gather(direction, 'row', axis=1, tiled=True)  204 us
    psum x2, blocking collectives, local(): curve = lax.psum(jnp.sum(direction * image, axis=1), ('region', 'row'))  202 us
    all_gather x1, waiting for transfers between devices, local(): region_scores = lax.all_gather(stored, 'row', axis=1, tiled=True)  85.5 us
    all_gather x1, blocking collectives, local(): all_queries = lax.all_gather(queries, 'row', axis=0, tiled=True)  32.4 us
  transfers between devices with their start and end apart: 10, of which 10 were waited for; matrix products, arithmetic and copies ran while one was open for 0% of the time, Pallas kernels for 0%

commit v1 on v0

--- a/solution.py
+++ b/solution.py
@@ -4,6 +4,11 @@
 from jax.sharding import PartitionSpec as P
 
 ITERS = 3
+
+
+def gather_from_all(value, axis, dim):
+    copies = jnp.concatenate([value] * lax.axis_size(axis), axis=dim)
+    return lax.all_to_all(copies, axis, dim, dim, tiled=True)
 
 
 def with_halo(block, sides, width):
@@ -65,7 +70,7 @@
     member = jnp.any(candidates[:, :, None] == own_blocks[None, None, :], axis=1)
     member_rows = jnp.repeat(member, tile_size, axis=1)
     stored = jnp.where(member_rows, jnp.exp(scores), jnp.float32(0.0))
-    region_scores = lax.all_gather(stored, "row", axis=1, tiled=True)
+    region_scores = gather_from_all(stored, "row", 1)
     seeds = jnp.take(region_scores, cluster_perm[0], axis=1)
     diffused = jnp.zeros_like(seeds)
     residual = seeds

time: 884 us -> 853 us (0.965)
  waiting for transfers between devices: 302 us -> 253 us
  starting transfers between devices: 7.3 us -> 25.5 us
    all_gather x1 -> x0, waiting for transfers between devices: 85.5 us -> none  [local(): region_scores = lax.all_gather(stored, 'row', axis=1, tiled=True)]
    all_to_all x0 -> x1, waiting for transfers between devices: none -> 37.2 us  [gather_from_all(): return lax.all_to_all(copies, axis, dim, dim, tiled=True)]
    ppermute x3, starting transfers between devices: 7.13 us -> 18.8 us  [with_halo(): lax.ppermute(lax.slice_in_dim(block, block.shape[dim] - width, None, axis...]
where the time goes in v1:
time: 853 us; the launch traced here: 852 us
  blocking collectives  525 us (62%)
  waiting for transfers between devices  253 us (30%)
  starting transfers between devices  25.5 us (3%)
  between operations  14.4 us (2%)
  local copies, waits for them, and re-layouts  12.9 us (2%)
  matrix products  11.3 us (1%)
  other arithmetic  10.7 us (1%)
    psum x3, blocking collectives, square_sum(): return lax.psum(jnp.sum(residual * residual, axis=1), ('region', 'row'))  290 us
    all_gather x3, waiting for transfers between devices, apply_operator(): region_field = lax.all_gather(direction, 'row', axis=1, tiled=True)  204 us
    psum x2, blocking collectives, local(): curve = lax.psum(jnp.sum(direction * image, axis=1), ('region', 'row'))  202 us
    all_to_all x1, waiting for transfers between devices, gather_from_all(): return lax.all_to_all(copies, axis, dim, dim, tiled=True)  37.2 us
    all_gather x1, blocking collectives, local(): all_queries = lax.all_gather(queries, 'row', axis=0, tiled=True)  32.4 us
    ppermute x3, starting transfers between devices, with_halo(): lax.ppermute(lax.slice_in_dim(block, block.shape[dim] - width, None, axis...  18.8 us
  transfers between devices with their start and end apart: 10, of which 10 were waited for; matrix products, arithmetic and copies ran while one was open for 0% of the time, Pallas kernels for 0%

profile of v1, /device:TPU:1, one launch (start us, length us, event | category | flops | bytes accessed | tf_op | source)
XLA Modules:
  0.0 852.4 jit_solution(1690045747724150492)
XLA Ops:
  8.3 32.4 %all-gather = f32[32,2,512]{2,1,0:T(2,128)S(1)} all-gather(f32[1,2,512]{2,1,0:T(2,128)} %bitcast.172), channel_id=1, replica_groups=mesh['region'=16,'row'=32] {'row'}, dimensions={0}, use_global_device_ids=true | all-gather | bytes 135168 | tf_op jit(solution)/shard_map/all_gather | solution.py:61
  40.9 1.7 constant_dynamic-update-slice_fusion.31
  43.1 1.6 copy.197
  44.6 6.6 all-to-all-start
  51.3 37.2 %all-to-all-done = f32[64,32,256]{2,0,1:T(8,128)S(1)} async-done(((f32[64,32,256]{2,0,1:T(8,128)}), f32[64,32,256]{2,0,1:T(8,128)S(1)}, u32[]{:S(2)}, u32[]{:S(2)}) %all-to-all-start) | async-done | bytes 2097184 | tf_op jit(solution)/shard_map/all_to_all | solution.py:11
  88.5 2.7 copy.88
  91.2 2.9 gather_fusion
  95.1 16.4 %collective-permute-start = (f32[1,64,256]{2,1,0:T(8,128)S(1)}, f32[1,64,256]{2,1,0:T(8,128)S(1)}, u32[]{:S(2)}, u32[]{:S(2)}) collective-permute-start(f32[1,64,256]{2,1,0:T(8,128)S(1)} %bitcast_select_fusion.1), channel_id=1, source_target_pairs={{0,32},{32,64},{64,96},{96,128},{128,160},{160,192},{192,224},{224... | collective-permute-start | bytes 196616 | tf_op jit(solution)/shard_map/ppermute | solution.py:20
  111.5 1.3 collective-permute-done
  112.8 2.4 collective-permute-done.1
  115.2 71.0 %all-gather.5.cloned.1.call-done = f32[64,8192]{1,0:T(8,128)} async-done(((f32[64,256]{1,0:T(8,128)}), f32[64,8192]{1,0:T(8,128)}) %all-gather.5.cloned.1.call-update) | async-done | bytes 2097168 | tf_op jit(solution)/shard_map/all_gather | solution.py:36
  186.2 1.9 bitcast_bitcast_fusion.2
  188.2 1.3 gather_fusion.1
  189.5 2.6 fusion.29
  192.9 101.1 %all-reduce = (f32[64]{0:T(128)S(1)}, f32[64]{0:T(128)S(1)}) all-reduce(f32[64]{0:T(128)S(1)} %get-tuple-element.16, f32[64]{0:T(128)S(1)} %multiply_reduce_fusion.3), channel_id=1, replica_groups=mesh['region'=16,'row'=32] {'region','row'}, use_global_device_ids=true, to_apply=%region_2.3 | all-reduce | flops 128 | bytes 1024 | tf_op jit(solution)/shard_map/psum | solution.py:51
  294.1 94.4 %psum.44 = f32[64]{0:T(128)S(1)} all-reduce(f32[64]{0:T(128)S(1)} %multiply_reduce_fusion.2), channel_id=1, replica_groups=mesh['region'=16,'row'=32] {'region','row'}, use_global_device_ids=true, to_apply=%region_6.7 | all-reduce | flops 64 | bytes 512 | tf_op jit(solution)/shard_map/psum | solution.py:51
  390.7 1.3 collective-permute-done.2
  392.1 2.7 collective-permute-done.3
  394.7 66.5 %all-gather.7.cloned.1.call-done = f32[64,8192]{1,0:T(8,128)} async-done(((f32[64,256]{1,0:T(8,128)}), f32[64,8192]{1,0:T(8,128)}) %all-gather.7.cloned.1.call-update) | async-done | bytes 2097168 | tf_op jit(solution)/shard_map/all_gather | solution.py:36
  461.3 1.9 bitcast_bitcast_fusion.1
  463.2 1.3 gather_fusion.2
  464.5 2.6 fusion.30
  467.9 101.1 %psum.45 = f32[64]{0:T(128)S(1)} all-reduce(f32[64]{0:T(128)S(1)} %multiply_reduce_fusion.1), channel_id=1, replica_groups=mesh['region'=16,'row'=32] {'region','row'}, use_global_device_ids=true, to_apply=%region_8.9 | all-reduce | flops 64 | bytes 512 | tf_op jit(solution)/shard_map/psum | solution.py:81
  569.2 94.6 %psum.46 = f32[64]{0:T(128)S(1)} all-reduce(f32[64]{0:T(128)S(1)} %multiply_reduce_fusion), channel_id=1, replica_groups=mesh['region'=16,'row'=32] {'region','row'}, use_global_device_ids=true, to_apply=%region_10.11 | all-reduce | flops 64 | bytes 512 | tf_op jit(solution)/shard_map/psum | solution.py:51
  665.4 1.2 collective-permute-start.4
  666.5 1.3 collective-permute-done.4
  667.9 2.7 collective-permute-done.5
  670.5 66.5 %all-gather.9.cloned.1.call-done = f32[64,8192]{1,0:T(8,128)} async-done(((f32[64,256]{1,0:T(8,128)}), f32[64,8192]{1,0:T(8,128)}) %all-gather.9.cloned.1.call-update) | async-done | bytes 2097168 | tf_op jit(solution)/shard_map/all_gather | solution.py:36
  737.1 1.9 bitcast_bitcast_fusion
  739.0 1.6 gather_fusion.3
  740.6 2.6 fusion.31
  744.1 101.1 %psum.47 = f32[64]{0:T(128)S(1)} all-reduce(f32[64]{0:T(128)S(1)} %fusion.8), channel_id=1, replica_groups=mesh['region'=16,'row'=32] {'region','row'}, use_global_device_ids=true, to_apply=%region_12.13 | all-reduce | flops 64 | bytes 512 | tf_op jit(solution)/shard_map/psum | solution.py:81
  (109 shorter events, 9.7 us)
Async XLA Ops:
  7.2 182.3 %copy-start = (f32[12,128,128]{2,1,0:T(8,128)S(1)}, f32[12,128,128]{2,1,0:T(8,128)}, u32[]{:S(2)}) copy-start(f32[12,128,128]{2,1,0:T(8,128)} %param.11) | copy-start | bytes 2359300
  44.6 6.6 copy-start.11
  44.6 43.9 %all-to-all-start = ((f32[64,32,256]{2,0,1:T(8,128)}), f32[64,32,256]{2,0,1:T(8,128)S(1)}, u32[]{:S(2)}, u32[]{:S(2)}) async-start(f32[64,32,256]{2,0,1:T(8,128)} %bitcast.162), calls=%async_computation | async-start | bytes 4194304 | tf_op jit(solution)/shard_map/all_to_all | solution.py:11
  51.2 135.0 %all-gather.5.cloned.1.call-start = ((), (), s32[]{:S(2)}) async-start(), calls=%async_computation.1 | async-start | bytes 2162688 | tf_op jit(solution)/shard_map/all_gather | solution.py:36
  51.3 338.2 %copy-start.4 = (pred[256]{0:T(512)(128)(4,1)}, pred[256]{0:T(512)(128)(4,1)S(1)}, u32[]{:S(2)}) copy-start(pred[256]{0:T(512)(128)(4,1)S(1)} %compare_and_fusion.1) | copy-start | bytes 772
  51.3 43.7 %copy-start.12 = (s32[12]{0:T(128)S(1)}, s32[12]{0:T(128)}, u32[]{:S(2)}) copy-start(s32[12]{0:T(128)} %param.13) | copy-start | bytes 148
  95.0 366.3 %all-gather.7.cloned.1.call-start = ((), (), s32[]{:S(2)}) async-start(), calls=%async_computation.2 | async-start | bytes 2162688 | tf_op jit(solution)/shard_map/all_gather | solution.py:36
  95.1 17.8 %collective-permute-start = (f32[1,64,256]{2,1,0:T(8,128)S(1)}, f32[1,64,256]{2,1,0:T(8,128)S(1)}, u32[]{:S(2)}, u32[]{:S(2)}) collective-permute-start(f32[1,64,256]{2,1,0:T(8,128)S(1)} %bitcast_select_fusion.1), channel_id=1, source_target_pairs={{0,32},{32,64},{64,96},{96,128},{128,160},{160,192},{192,224},{224... | collective-permute-start | bytes 196616 | tf_op jit(solution)/shard_map/ppermute | solution.py:20
  111.5 3.7 collective-permute-start.1
  111.5 351.6 %copy-start.6 = (s32[1024]{0:T(1024)}, s32[1024]{0:T(1024)S(1)}, u32[]{:S(2)}) copy-start(s32[1024]{0:T(1024)S(1)} %pad_clamp_fusion) | copy-start | bytes 12292
  188.1 4.0 copy-start.9
  188.1 200.4 %copy-start.1 = (f32[64,256]{1,0:T(8,128)S(1)}, f32[64,256]{1,0:T(8,128)}, u32[]{:S(2)}) copy-start(f32[64,256]{1,0:T(8,128)} %get-tuple-element.17) | copy-start | bytes 196612
  389.3 347.8 %all-gather.9.cloned.1.call-start = ((), (), s32[]{:S(2)}) async-start(), calls=%async_computation.3 | async-start | bytes 2162688 | tf_op jit(solution)/shard_map/all_gather | solution.py:36
  389.6 2.5 collective-permute-start.2
  390.7 4.0 collective-permute-start.3
  463.1 201.2 %copy-start.2 = (f32[64,256]{1,0:T(8,128)S(1)}, f32[64,256]{1,0:T(8,128)}, u32[]{:S(2)}) copy-start(f32[64,256]{1,0:T(8,128)} %multiply_add_fusion.4) | copy-start | bytes 196612
  464.5 200.8 %copy-start.5 = (pred[256]{0:T(512)(128)(4,1)S(1)}, pred[256]{0:T(512)(128)(4,1)}, u32[]{:S(2)}) copy-start(pred[256]{0:T(512)(128)(4,1)} %copy-done.4) | copy-start | bytes 772
  663.8 0.6 copy-start.13
  664.4 72.7 %copy-start.7 = (f32[64]{0:T(128)}, f32[64]{0:T(128)S(1)}, u32[]{:S(2)}) copy-start(f32[64]{0:T(128)S(1)} %div.18) | copy-start | bytes 772
  665.4 2.5 collective-permute-start.4
  666.5 4.0 collective-permute-start.5
  739.0 4.3 copy-start.10
  739.0 4.9 copy-start.8
  739.0 106.2 %copy-start.14 = (f32[64]{0:T(128)S(1)}, f32[64]{0:T(128)}, u32[]{:S(2)}) copy-start(f32[64]{0:T(128)} %copy-done.13) | copy-start | bytes 772
  739.0 106.2 %copy-start.3 = (f32[64,256]{1,0:T(8,128)S(1)}, f32[64,256]{1,0:T(8,128)}, u32[]{:S(2)}) copy-start(f32[64,256]{1,0:T(8,128)} %get-tuple-element.14) | copy-start | bytes 196612
Sparse Core Ops, SparseCore 0:
  95.1 91.1 all-gather.4
  389.4 71.7 all-gather.6
  665.3 71.7 all-gather.8
